TPU v7x, 32 devices: a whole 2x2x4 slice. The times are simulated.
32 devices in a mesh: fsdp: 4 (over z), ty: 4 (over y, core), tx: 2 (over x).
Axes of the slice: x: 2, y: 2, z: 4, core: 2. Of those that a mesh axis runs over, the one named last changes fastest.
Arguments:
- q_raw: bfloat16 [8, 32, 16, 1536], P('fsdp', 'ty', 'tx'), may hold values from -6 to 6
- k_raw: bfloat16 [8, 32, 16, 1536], P('fsdp', 'ty', 'tx'), may hold values from -6 to 6
- values: bfloat16 [8, 32, 16, 1536], P('fsdp', 'ty', 'tx'), may hold values from -6 to 6
- d_out: bfloat16 [8, 32, 16, 1536], P('fsdp', 'ty', 'tx'), may hold values from -6 to 6
- q_gain: float32 [128], P('fsdp'), may hold values from 0.1 to 1.9
- k_gain: float32 [128], P('fsdp'), may hold values from 0.1 to 1.9
- windows: int32 [12, 2], replicated, may hold values from 1 to 3, as said below
Outputs:
- out: bfloat16 [8, 32, 16, 1536], P('fsdp', 'ty', 'tx')
- q_grad: bfloat16 [8, 32, 16, 1536], P('fsdp', 'ty', 'tx')
- k_grad: bfloat16 [8, 32, 16, 1536], P('fsdp', 'ty', 'tx')
- v_grad: bfloat16 [8, 32, 16, 1536], P('fsdp', 'ty', 'tx')
- q_gain_grad: float32 [128], P('fsdp')
- k_gain_grad: float32 [128], P('fsdp')
Inputs may be any that keep to these rules, and one draw needn't show every extreme that they name: `windows`: every entry is 1 or 3; in each of the two columns some head has 3.
All inputs are finite; a program needn't handle non-finite values.
Results may differ from a plain program's by a relative error of at most 0.0083.
Values may be sent and summed in bfloat16 or wider, within the bound.
A program may use at most 64 MiB of HBM per device.

v0:
```python
import math

import jax
import jax.numpy as jnp
from jax import lax
from jax.sharding import PartitionSpec as P

TILE = 8


NORM_EPS = 1e-06


def padded(cells, sides, width):
    for axis, dim in sides:
        count = lax.axis_size(axis)
        ends = count - 1
        head = lax.slice_in_dim(cells, 0, width, axis=dim)
        tail = lax.slice_in_dim(cells, cells.shape[dim] - width, cells.shape[dim], axis=dim)
        cells = jnp.concatenate(
            [
                lax.ppermute(tail, axis, [(i, (i + 1) % count) for i in range(ends)]),
                cells,
                lax.ppermute(head, axis, [((i + 1) % count, i) for i in range(ends)]),
            ],
            axis=dim,
        )
    return cells


def product(form, left, right):
    return jnp.einsum(form, left, right, preferred_element_type=jnp.float32)


def normalize(raw_field, norm_gain, head_count):
    floats = raw_field.astype(jnp.float32)
    floats = floats.reshape(floats.shape[:-1] + (head_count, norm_gain.shape[0]))
    inverse = lax.rsqrt(jnp.mean(floats * floats, axis=-1, keepdims=True) + NORM_EPS)
    normed = floats * inverse
    return (normed, inverse, (normed * norm_gain).astype(jnp.bfloat16))


def norm_backward(upstream, normed, inverse, norm_gain):
    gain_part = jnp.sum(upstream * normed, axis=tuple(range(upstream.ndim - 1)))
    scaled = upstream * norm_gain
    raw_grad = inverse * (scaled - normed * jnp.mean(scaled * normed, axis=-1, keepdims=True))
    return (raw_grad, gain_part)


def open_pairs(windows, tile_size):
    span = 3 * tile_size
    spots = jnp.arange(span * span, dtype=jnp.int32)
    step_rows = spots // span // tile_size - 1
    step_cols = spots % span // tile_size - 1
    tile_row = lax.axis_index("ty") + step_rows
    tile_col = lax.axis_index("tx") + step_cols
    inside = (
        (tile_row >= 0)
        & (tile_row < lax.axis_size("ty"))
        & (tile_col >= 0)
        & (tile_col < lax.axis_size("tx"))
    )
    reach_rows = ((windows[:, 0] - 1) // 2)[:, None]
    reach_cols = ((windows[:, 1] - 1) // 2)[:, None]
    within = (jnp.abs(step_rows)[None, :] <= reach_rows) & (
        jnp.abs(step_cols)[None, :] <= reach_cols
    )
    return inside[None, :] & within


def query_side(queries, keys_near, values_near, grad_out, open_mask, score_scale):
    scores = product("qhc,mhc->hqm", queries, keys_near) * score_scale
    weights = jnp.where(open_mask[:, None, :], jnp.exp(scores), 0.0)
    totals = jnp.sum(weights, axis=2)
    shares = weights / totals[:, :, None]
    shares_low = shares.astype(jnp.bfloat16)
    output = product("hqm,mhc->qhc", shares_low, values_near).astype(jnp.bfloat16)
    output_back = lax.optimization_barrier(output).astype(jnp.float32)
    row_delta = jnp.sum(grad_out.astype(jnp.float32) * output_back, axis=-1)
    share_grad = product("qhc,mhc->hqm", grad_out, values_near)
    score_grad = (shares * (share_grad - row_delta.T[:, :, None])).astype(jnp.bfloat16)
    query_grad = product("hqm,mhc->qhc", score_grad, keys_near) * score_scale
    return (output, totals.T, row_delta, query_grad)


def key_side(
    keys, value_rows, queries_near, grads_near, totals_near, delta_near, open_mask, score_scale
):
    scores = product("khc,mhc->hkm", keys, queries_near) * score_scale
    mask_rows = open_mask[:, None, :]
    weights = jnp.where(mask_rows, jnp.exp(scores), 0.0)
    divisor = jnp.where(open_mask, totals_near.T, 1.0)[:, None, :]
    shares = weights / divisor
    shares_low = shares.astype(jnp.bfloat16)
    value_grad = product("hkm,mhc->khc", shares_low, grads_near)
    share_grad = product("mhc,khc->hkm", grads_near, value_rows)
    score_grad = (shares * (share_grad - delta_near.T[:, None, :])).astype(jnp.bfloat16)
    key_grad = product("hkm,mhc->khc", score_grad, queries_near) * score_scale
    return (key_grad, value_grad)


def body(q_raw, k_raw, values, d_out, q_gain, k_gain, windows):
    head_count = windows.shape[0]
    q_gain_all, k_gain_all = (
        lax.all_gather(q_gain, "fsdp", axis=0, tiled=True),
        lax.all_gather(k_gain, "fsdp", axis=0, tiled=True),
    )
    frame_count, row_count, col_count, feature_count = q_raw.shape
    head_size = q_gain_all.shape[0]
    score_scale = 1.0 / math.sqrt(head_size)
    q_normed, q_inverse, q_hat = normalize(q_raw, q_gain_all, head_count)
    k_normed, k_inverse, k_hat = normalize(k_raw, k_gain_all, head_count)
    q_flat = q_hat.reshape(q_raw.shape)
    k_flat = k_hat.reshape(k_raw.shape)
    open_mask = open_pairs(windows, TILE)
    local_rows = row_count * col_count
    near_rows = (row_count + 2 * TILE) * (col_count + 2 * TILE)

    def as_local(field):
        return field.reshape(frame_count, local_rows, head_count, head_size)

    def as_near(field):
        return field.reshape(frame_count, near_rows, head_count, head_size)

    arrived = padded(jnp.stack([k_flat, values]), (("ty", 2), ("tx", 3)), TILE)

    def frame_query(queries, keys_near, values_near, grad_out):
        return query_side(queries, keys_near, values_near, grad_out, open_mask, score_scale)

    output, totals, row_delta, query_grad = jax.vmap(frame_query)(
        as_local(q_flat), as_near(arrived[0]), as_near(arrived[1]), as_local(d_out)
    )
    stat_grid = jnp.stack([totals, row_delta]).reshape(
        2, frame_count, row_count, col_count, head_count
    )
    row_sums = padded(stat_grid, (("ty", 2), ("tx", 3)), TILE)
    row_sums = row_sums.reshape(2, frame_count, near_rows, head_count)
    arrived_back = padded(jnp.stack([q_flat, d_out]), (("ty", 2), ("tx", 3)), TILE)
    query_fields = arrived_back[0]
    grad_fields = arrived_back[1]

    def frame_key(keys, value_rows, queries_near, grads_near, totals_near, delta_near):
        return key_side(
            keys,
            value_rows,
            queries_near,
            grads_near,
            totals_near,
            delta_near,
            open_mask,
            score_scale,
        )

    key_grad, value_grad = jax.vmap(frame_key)(
        as_local(k_flat),
        as_local(values),
        as_near(query_fields),
        as_near(grad_fields),
        row_sums[0],
        row_sums[1],
    )
    q_upstream = query_grad.reshape(q_normed.shape)
    k_upstream = key_grad.reshape(k_normed.shape)
    q_field_grad, q_part = norm_backward(q_upstream, q_normed, q_inverse, q_gain_all)
    k_field_grad, k_part = norm_backward(k_upstream, k_normed, k_inverse, k_gain_all)
    gain_parts = jnp.stack([q_part, k_part])
    whole_sum = lax.psum(gain_parts, ("fsdp", "ty", "tx"))
    share_len = whole_sum.shape[1] // lax.axis_size("fsdp")
    owned = lax.dynamic_slice_in_dim(whole_sum, lax.axis_index("fsdp") * share_len, share_len, 1)
    return (
        output.reshape(q_raw.shape),
        q_field_grad.reshape(q_raw.shape).astype(jnp.bfloat16),
        k_field_grad.reshape(k_raw.shape).astype(jnp.bfloat16),
        value_grad.reshape(values.shape).astype(jnp.bfloat16),
        owned[0],
        owned[1],
    )


def solution(mesh):
    return jax.shard_map(
        body,
        mesh=mesh,
        in_specs=(
            P("fsdp", "ty", "tx", None),
            P("fsdp", "ty", "tx", None),
            P("fsdp", "ty", "tx", None),
            P("fsdp", "ty", "tx", None),
            P("fsdp"),
            P("fsdp"),
            P(),
        ),
        out_specs=(
            P("fsdp", "ty", "tx", None),
            P("fsdp", "ty", "tx", None),
            P("fsdp", "ty", "tx", None),
            P("fsdp", "ty", "tx", None),
            P("fsdp"),
            P("fsdp"),
        ),
        check_vma=False,
    )
```

profile of v0, /device:TPU:0, one launch (start us, length us, event | category | flops | bytes accessed | tf_op | source)
XLA Modules:
  0.0 281.0 jit_solution(18281681480444899220)
XLA Ops:
  0.7 1.3 bitcast_reduce_fusion.1
  2.0 1.3 dynamic-slice
  5.7 13.4 %all-reduce.2 = (f32[128]{0:T(128)S(1)}, f32[128]{0:T(128)S(1)}) all-reduce(f32[128]{0:T(128)S(1)} %dynamic-update-slice, f32[128]{0:T(128)S(1)} %dynamic-update-slice.1), channel_id=1, replica_groups=mesh['fsdp'=4,'ty'=4,'tx'=2] {'fsdp'}, use_global_device_ids=true, to_apply=%add | all-reduce | flops 256 | bytes 2048
  19.1 1.3 fusion.64
  21.5 1.4 collective-permute-start.1
  22.9 3.1 %collective-permute-start = (bf16[2,2,8,8,1536]{4,3,2,1,0:T(8,128)(2,1)S(1)}, bf16[2,2,8,8,1536]{4,3,2,1,0:T(8,128)(2,1)S(1)}, u32[]{:S(2)}, u32[]{:S(2)}) collective-permute-start(bf16[2,2,8,8,1536]{4,3,2,1,0:T(8,128)(2,1)S(1)} %pad_maximum_fusion.4), channel_id=1, source_target_pairs={{0,2},{2,4},{4,6},{1,3},{3,5},{5,7},{8,10},{10,12},{12,14},{9,11},... | collective-permute-start | bytes 2359304 | tf_op jit(solution)/shard_map/ppermute | solution.py:22
  26.0 1.8 collective-permute-done
  27.9 2.7 pad_maximum_fusion.2
  30.6 1.3 collective-permute-start.3
  31.9 7.4 %collective-permute-start.2 = (bf16[2,2,24,8,1536]{4,3,2,1,0:T(8,128)(2,1)}, bf16[2,2,24,8,1536]{4,3,2,1,0:T(8,128)(2,1)}, u32[]{:S(2)}, u32[]{:S(2)}) collective-permute-start(bf16[2,2,24,8,1536]{4,3,2,1,0:T(8,128)(2,1)} %pad_maximum_fusion.2), channel_id=1, source_target_pairs={{0,1},{2,3},{4,5},{6,7},{8,9},{10,11},{12,13},{14,15},{16,17},{18,... | collective-permute-start | bytes 7077896 | tf_op jit(solution)/shard_map/ppermute | solution.py:22
  39.3 1.2 reshape.213
  43.9 35.7 %collective-permute-done.3 = bf16[2,2,24,8,1536]{4,3,2,1,0:T(8,128)(2,1)} collective-permute-done((bf16[2,2,24,8,1536]{4,3,2,1,0:T(8,128)(2,1)}, bf16[2,2,24,8,1536]{4,3,2,1,0:T(8,128)(2,1)}, u32[]{:S(2)}, u32[]{:S(2)}) %collective-permute-start.3) | collective-permute-done | bytes 2359328 | tf_op jit(solution)/shard_map/ppermute | solution.py:24
  79.6 3.2 %collective-permute-done.2 = bf16[2,2,24,8,1536]{4,3,2,1,0:T(8,128)(2,1)} collective-permute-done((bf16[2,2,24,8,1536]{4,3,2,1,0:T(8,128)(2,1)}, bf16[2,2,24,8,1536]{4,3,2,1,0:T(8,128)(2,1)}, u32[]{:S(2)}, u32[]{:S(2)}) %collective-permute-start.2) | collective-permute-done | bytes 2359328 | tf_op jit(solution)/shard_map/ppermute | solution.py:22
  82.8 3.3 %pad_maximum_fusion = bf16[2,2,24,24,1536]{4,3,2,1,0:T(8,128)(2,1)S(1)} fusion(bf16[2,2,24,8,1536]{4,3,2,1,0:T(8,128)(2,1)} %collective-permute-done.3, bf16[2,2,8,8,1536]{4,3,2,1,0:T(8,128)(2,1)S(1)} %collective-permute-done.1, bf16[1,2,8,8,1536]{4,3,2,1,0:T(8,128)(2,1)S(1)} %bitcast.140, bf16[1,2,8,8,1536]{4,3,2,1,0:T(8,128)(2,1)S(1)} %fusion.64, ...), kind=kLoop, calls=%fused_computation | loop fusion | flops 42467328 | bytes 14155776 | tf_op jit(solution)/shard_map/concatenate | solution.py:20
  86.1 2.5 fusion.97
  88.5 7.4 %reshape_squeeze.12 = bf16[2,576,12,128]{3,2,1,0:T(8,128)(2,1)} reshape(bf16[1,2,24,24,1536]{4,3,2,1,0:T(8,128)(2,1)} %get-tuple-element.15) | data formatting | bytes 7077888 | tf_op jit(solution)/shard_map/reshape;squeeze | solution.py:123
  95.9 4.4 %reshape_squeeze.13 = bf16[2,576,12,128]{3,2,1,0:T(8,128)(2,1)} reshape(bf16[1,2,24,24,1536]{4,3,2,1,0:T(8,128)(2,1)S(1)} %get-tuple-element.14) | data formatting | bytes 7077888 | tf_op jit(solution)/shard_map/reshape;squeeze | solution.py:123
  100.3 5.6 %fusion.3 = (f32[2,12,64]{2,1,0:T(8,128)S(1)}, f32[2,12,64,576]{3,2,1,0:T(8,128)S(1)}) fusion(pred[12,576]{1,0:T(8,128)(4,1)} %and_and_fusion, bf16[2,576,12,128]{3,2,1,0:T(8,128)(2,1)} %reshape_squeeze.13, f32[128]{0:T(128)} %copy-done.27, f32[2,64,12]{1,2,0:T(8,128)} %reshape.230, f32[2,64,12,128]{3,2,1,0:T(8,128)} %reshape.213), kind=kOutput, calls=%fused_computation.9 | convolution fusion | flops 229734912 | bytes 7884032 | tf_op jit(solution)/shard_map/vmap(qhc,mhc->hqm)/dot_general | solution.py:32
  106.0 2.7 fusion.51
  109.8 9.2 %multiply_reduce_fusion.1 = (f32[128]{0:T(128)}, f32[2,64,12]{1,2,0:T(8,128)S(1)}, f32[2,12,128,64]{2,3,1,0:T(8,128)S(1)}) fusion(f32[2,64,12]{1,2,0:T(8,128)S(1)} %copy-done.24, f32[2,64,12,128]{3,2,1,0:T(8,128)S(1)} %copy-done.19, f32[128]{0:T(128)S(1)} %copy-done.31, bf16[2,576,12,128]{3,2,1,0:T(8,128)(2,1)} %reshape_squeeze.13, ...), kind=kOutput, calls=%fused_computation.57 | convolution fusion | flops 459667840 | bytes 12615424 | tf_op jit(solution)/shard_map/vmap(hqm,mhc->qhc)/dot_general | solution.py:32
  119.9 1.2 fusion.65
  121.3 1.4 collective-permute-start.5
  122.7 9.7 %collective-permute-start.4 = (bf16[2,2,8,8,1536]{4,3,2,1,0:T(8,128)(2,1)S(1)}, bf16[2,2,8,8,1536]{4,3,2,1,0:T(8,128)(2,1)S(1)}, u32[]{:S(2)}, u32[]{:S(2)}) collective-permute-start(bf16[2,2,8,8,1536]{4,3,2,1,0:T(8,128)(2,1)S(1)} %pad_maximum_fusion.5), channel_id=1, source_target_pairs={{0,2},{2,4},{4,6},{1,3},{3,5},{5,7},{8,10},{10,12},{12,14},{9,11},... | collective-permute-start | bytes 2359304 | tf_op jit(solution)/shard_map/ppermute | solution.py:22
  132.4 1.8 collective-permute-done.4
  134.2 1.7 pad_maximum_fusion.3
  135.9 1.3 collective-permute-start.7
  137.2 7.4 %collective-permute-start.6 = (bf16[2,2,24,8,1536]{4,3,2,1,0:T(8,128)(2,1)}, bf16[2,2,24,8,1536]{4,3,2,1,0:T(8,128)(2,1)}, u32[]{:S(2)}, u32[]{:S(2)}) collective-permute-start(bf16[2,2,24,8,1536]{4,3,2,1,0:T(8,128)(2,1)} %pad_maximum_fusion.3), channel_id=1, source_target_pairs={{0,1},{2,3},{4,5},{6,7},{8,9},{10,11},{12,13},{14,15},{16,17},{18,... | collective-permute-start | bytes 7077896 | tf_op jit(solution)/shard_map/ppermute | solution.py:22
  146.2 1.3 collective-permute-start.9
  147.5 11.4 %collective-permute-start.8 = (f32[2,2,8,8,12]{3,2,1,4,0:T(8,128)}, f32[2,2,8,8,12]{3,2,1,4,0:T(8,128)}, u32[]{:S(2)}, u32[]{:S(2)}) collective-permute-start(f32[2,2,8,8,12]{3,2,1,4,0:T(8,128)} %constant_dynamic-update-slice_fusion), channel_id=1, source_target_pairs={{0,2},{2,4},{4,6},{1,3},{3,5},{5,7},{8,10},{10,12},{12,14},{9,11},... | collective-permute-start | bytes 36872 | tf_op jit(solution)/shard_map/ppermute | solution.py:22
  160.0 1.7 copy.59
  161.7 1.7 copy.57
  163.4 1.9 pad_maximum_fusion.7
  165.3 1.3 collective-permute-start.11
  166.6 5.9 %collective-permute-start.10 = (f32[2,2,24,8,12]{2,3,4,1,0:T(8,128)}, f32[2,2,24,8,12]{2,3,4,1,0:T(8,128)}, u32[]{:S(2)}, u32[]{:S(2)}) collective-permute-start(f32[2,2,24,8,12]{2,3,4,1,0:T(8,128)} %pad_maximum_fusion.7), channel_id=1, source_target_pairs={{0,1},{2,3},{4,5},{6,7},{8,9},{10,11},{12,13},{14,15},{16,17},{18,... | collective-permute-start | bytes 110600 | tf_op jit(solution)/shard_map/ppermute | solution.py:22
  175.4 1.6 reshape.232
  177.0 1.3 copy.43
  179.3 9.3 %collective-permute-done.11 = f32[2,2,24,8,12]{2,3,4,1,0:T(8,128)} collective-permute-done((f32[2,2,24,8,12]{2,3,4,1,0:T(8,128)}, f32[2,2,24,8,12]{2,3,4,1,0:T(8,128)}, u32[]{:S(2)}, u32[]{:S(2)}) %collective-permute-start.11) | collective-permute-done | bytes 36896 | tf_op jit(solution)/shard_map/ppermute | solution.py:24
  188.6 3.2 %collective-permute-done.10 = f32[2,2,24,8,12]{2,3,4,1,0:T(8,128)} collective-permute-done((f32[2,2,24,8,12]{2,3,4,1,0:T(8,128)}, f32[2,2,24,8,12]{2,3,4,1,0:T(8,128)}, u32[]{:S(2)}, u32[]{:S(2)}) %collective-permute-start.10) | collective-permute-done | bytes 36896 | tf_op jit(solution)/shard_map/ppermute | solution.py:22
  191.8 1.4 pad_maximum_fusion.6
  196.9 3.3 %pad_maximum_fusion.1 = bf16[2,2,24,24,1536]{4,3,2,1,0:T(8,128)(2,1)S(1)} fusion(bf16[2,2,24,8,1536]{4,3,2,1,0:T(8,128)(2,1)} %collective-permute-done.7, bf16[2,2,8,8,1536]{4,3,2,1,0:T(8,128)(2,1)S(1)} %collective-permute-done.5, bf16[1,2,8,8,1536]{4,3,2,1,0:T(8,128)(2,1)S(1)} %bitcast.143, bf16[1,2,8,8,1536]{4,3,2,1,0:T(8,128)(2,1)S(1)} %get-tuple-element.18, ...), kind=kLoop, calls=%fused_computation.1 | loop fusion | flops 42467328 | bytes 14155776 | tf_op jit(solution)/shard_map/concatenate | solution.py:20
  200.2 2.5 fusion.96
  202.6 7.4 %reshape_squeeze.14 = bf16[2,576,12,128]{3,2,1,0:T(8,128)(2,1)} reshape(bf16[1,2,24,24,1536]{4,3,2,1,0:T(8,128)(2,1)} %get-tuple-element.13) | data formatting | bytes 7077888 | tf_op jit(solution)/shard_map/reshape;squeeze | solution.py:123
  210.0 4.4 %reshape_squeeze.15 = bf16[2,576,12,128]{3,2,1,0:T(8,128)(2,1)} reshape(bf16[1,2,24,24,1536]{4,3,2,1,0:T(8,128)(2,1)S(1)} %get-tuple-element.12) | data formatting | bytes 7077888 | tf_op jit(solution)/shard_map/reshape;squeeze | solution.py:123
  214.4 5.3 %select_divide_fusion = f32[2,12,64,576]{3,2,1,0:T(8,128)S(1)} fusion(f32[2,12,576]{2,1,0:T(8,128)} %copy.61, pred[12,576]{1,0:T(8,128)(4,1)} %and_and_fusion, bf16[2,576,12,128]{3,2,1,0:T(8,128)(2,1)} %reshape_squeeze.14, f32[128]{0:T(128)S(1)} %copy-done.26, f32[2,64,12,128]{3,2,1,0:T(8,128)} %reshape.217, f32[2,64,12]{1,2,0:T(8,128)} %reshape.232), kind=kOutput, calls=%fused_computation.6 | convolution fusion | flops 229736448 | bytes 7933184 | tf_op jit(solution)/shard_map/vmap(khc,mhc->hkm)/dot_general | solution.py:32
  219.8 1.7 fusion.46
  222.4 8.9 %multiply_reduce_fusion = (f32[128]{0:T(128)S(1)}, f32[2,64,12]{1,2,0:T(8,128)S(1)}, f32[2,12,128,64]{2,3,1,0:T(8,128)S(1)}) fusion(f32[2,64,12]{1,2,0:T(8,128)S(1)} %copy-done.23, f32[2,64,12,128]{3,2,1,0:T(8,128)S(1)} %copy-done.18, f32[128]{0:T(128)S(1)} %copy-done.29, bf16[2,576,12,128]{3,2,1,0:T(8,128)(2,1)} %reshape_squeeze.14, ...), kind=kOutput, calls=%fused_computation.56 | convolution fusion | flops 457013632 | bytes 12651520 | tf_op jit(solution)/shard_map/vmap(hkm,mhc->khc)/dot_general | solution.py:32
  233.4 45.7 %psum.7 = f32[2,128]{1,0:T(2,128)S(1)} all-reduce(f32[2,128]{1,0:T(2,128)S(1)} %pad_maximum_fusion.8), channel_id=1, replica_groups=mesh['fsdp'=4,'ty'=4,'tx'=2] {'fsdp','ty','tx'}, use_global_device_ids=true, to_apply=%region_8.9 | all-reduce | flops 256 | bytes 2048 | tf_op jit(solution)/shard_map/psum | solution.py:167
  279.7 1.2 fusion.58
  (127 shorter events, 22.0 us)
Async XLA Ops:
  0.6 38.7 %copy-start.9 = (bf16[2,8,8,1536]{3,2,1,0:T(8,128)(2,1)S(1)}, bf16[2,8,8,1536]{3,2,1,0:T(8,128)(2,1)}, u32[]{:S(2)}) copy-start(bf16[2,8,8,1536]{3,2,1,0:T(8,128)(2,1)} %param.7) | copy-start | bytes 1179652
  2.0 18.4 %copy-start.11 = (f32[2,8,8,12]{2,3,1,0:T(8,128)}, f32[2,8,8,12]{2,3,1,0:T(8,128)S(1)}, u32[]{:S(2)}) copy-start(f32[2,8,8,12]{2,3,1,0:T(8,128)S(1)} %add_rsqrt_fusion.1) | copy-start | bytes 18436
  19.1 23.6 %copy-start.25 = (f32[128]{0:T(128)}, f32[128]{0:T(128)S(1)}, u32[]{:S(2)}) copy-start(f32[128]{0:T(128)S(1)} %get-tuple-element.10) | copy-start | bytes 1540
  19.1 23.6 %copy-start.27 = (f32[128]{0:T(128)}, f32[128]{0:T(128)S(1)}, u32[]{:S(2)}) copy-start(f32[128]{0:T(128)S(1)} %get-tuple-element.11) | copy-start | bytes 1540
  21.5 20.1 %copy-start.3 = (bf16[2,8,8,1536]{3,2,1,0:T(8,128)(2,1)S(1)}, bf16[2,8,8,1536]{3,2,1,0:T(8,128)(2,1)}, u32[]{:S(2)}) copy-start(bf16[2,8,8,1536]{3,2,1,0:T(8,128)(2,1)} %param.10) | copy-start | bytes 1179652
  21.5 21.7 %copy-start.28 = (s32[12,2]{0,1:T(2,128)S(1)}, s32[12,2]{0,1:T(2,128)}, u32[]{:S(2)}) copy-start(s32[12,2]{0,1:T(2,128)} %param.13) | copy-start | bytes 292
  21.5 61.3 %copy-start.1 = (bf16[2,8,8,1536]{3,2,1,0:T(8,128)(2,1)S(1)}, bf16[2,8,8,1536]{3,2,1,0:T(8,128)(2,1)}, u32[]{:S(2)}) copy-start(bf16[2,8,8,1536]{3,2,1,0:T(8,128)(2,1)} %param.9) | copy-start | bytes 1179652
  21.5 4.5 %collective-permute-start.1 = (bf16[2,2,8,8,1536]{4,3,2,1,0:T(8,128)(2,1)S(1)}, bf16[2,2,8,8,1536]{4,3,2,1,0:T(8,128)(2,1)S(1)}, u32[]{:S(2)}, u32[]{:S(2)}) collective-permute-start(bf16[2,2,8,8,1536]{4,3,2,1,0:T(8,128)(2,1)S(1)} %pad_maximum_fusion.4), channel_id=1, source_target_pairs={{2,0},{4,2},{6,4},{3,1},{5,3},{7,5},{10,8},{12,10},{14,12},{11,9},... | collective-permute-start | bytes 2359304 | tf_op jit(solution)/shard_map/ppermute | solution.py:24
  22.9 4.9 %collective-permute-start = (bf16[2,2,8,8,1536]{4,3,2,1,0:T(8,128)(2,1)S(1)}, bf16[2,2,8,8,1536]{4,3,2,1,0:T(8,128)(2,1)S(1)}, u32[]{:S(2)}, u32[]{:S(2)}) collective-permute-start(bf16[2,2,8,8,1536]{4,3,2,1,0:T(8,128)(2,1)S(1)} %pad_maximum_fusion.4), channel_id=1, source_target_pairs={{0,2},{2,4},{4,6},{1,3},{3,5},{5,7},{8,10},{10,12},{12,14},{9,11},... | collective-permute-start | bytes 2359304 | tf_op jit(solution)/shard_map/ppermute | solution.py:22
  30.6 49.1 %collective-permute-start.3 = (bf16[2,2,24,8,1536]{4,3,2,1,0:T(8,128)(2,1)}, bf16[2,2,24,8,1536]{4,3,2,1,0:T(8,128)(2,1)}, u32[]{:S(2)}, u32[]{:S(2)}) collective-permute-start(bf16[2,2,24,8,1536]{4,3,2,1,0:T(8,128)(2,1)} %pad_maximum_fusion.2), channel_id=1, source_target_pairs={{1,0},{3,2},{5,4},{7,6},{9,8},{11,10},{13,12},{15,14},{17,16},{19,... | collective-permute-start | bytes 7077896 | tf_op jit(solution)/shard_map/ppermute | solution.py:24
  31.9 50.9 %collective-permute-start.2 = (bf16[2,2,24,8,1536]{4,3,2,1,0:T(8,128)(2,1)}, bf16[2,2,24,8,1536]{4,3,2,1,0:T(8,128)(2,1)}, u32[]{:S(2)}, u32[]{:S(2)}) collective-permute-start(bf16[2,2,24,8,1536]{4,3,2,1,0:T(8,128)(2,1)} %pad_maximum_fusion.2), channel_id=1, source_target_pairs={{0,1},{2,3},{4,5},{6,7},{8,9},{10,11},{12,13},{14,15},{16,17},{18,... | collective-permute-start | bytes 7077896 | tf_op jit(solution)/shard_map/ppermute | solution.py:22
  40.8 42.0 %copy-start.16 = (f32[2,8,8,12]{2,3,1,0:T(8,128)}, f32[2,8,8,12]{2,3,1,0:T(8,128)S(1)}, u32[]{:S(2)}) copy-start(f32[2,8,8,12]{2,3,1,0:T(8,128)S(1)} %add_rsqrt_fusion) | copy-start | bytes 18436
  100.3 5.6 %copy-start.7 = (bf16[2,576,12,128]{3,2,1,0:T(8,128)(2,1)S(1)}, bf16[2,576,12,128]{3,2,1,0:T(8,128)(2,1)}, u32[]{:S(2)}) copy-start(bf16[2,576,12,128]{3,2,1,0:T(8,128)(2,1)} %reshape_squeeze.12) | copy-start | bytes 10616836
  100.3 5.6 %copy-start.22 = (pred[12,576]{1,0:T(8,128)(4,1)S(1)}, pred[12,576]{1,0:T(8,128)(4,1)}, u32[]{:S(2)}) copy-start(pred[12,576]{1,0:T(8,128)(4,1)} %and_and_fusion) | copy-start | bytes 20740
  105.9 2.8 copy-start.32
  105.9 3.5 %copy-start.14 = (bf16[2,64,12,128]{3,2,1,0:T(8,128)(2,1)S(1)}, bf16[2,64,12,128]{3,2,1,0:T(8,128)(2,1)}, u32[]{:S(2)}) copy-start(bf16[2,64,12,128]{3,2,1,0:T(8,128)(2,1)} %reshape.215) | copy-start | bytes 1179652
  105.9 3.8 %copy-start.19 = (f32[2,64,12,128]{3,2,1,0:T(8,128)S(1)}, f32[2,64,12,128]{3,2,1,0:T(8,128)}, u32[]{:S(2)}) copy-start(f32[2,64,12,128]{3,2,1,0:T(8,128)} %reshape.213) | copy-start | bytes 2359300
  106.0 3.8 %copy-start.24 = (f32[2,64,12]{1,2,0:T(8,128)S(1)}, f32[2,64,12]{1,2,0:T(8,128)}, u32[]{:S(2)}) copy-start(f32[2,64,12]{1,2,0:T(8,128)} %reshape.230) | copy-start | bytes 18436
  106.0 3.8 %copy-start.31 = (f32[128]{0:T(128)S(1)}, f32[128]{0:T(128)}, u32[]{:S(2)}) copy-start(f32[128]{0:T(128)} %get-tuple-element.31) | copy-start | bytes 1540
  108.7 0.7 copy-start.15
  118.9 1.0 copy-start.10
  118.9 1.0 copy-start.17
  118.9 2.2 copy-start.4
  121.3 51.2 %copy-start.12 = (f32[2,8,8,12]{2,3,1,0:T(8,128)S(1)}, f32[2,8,8,12]{2,3,1,0:T(8,128)}, u32[]{:S(2)}) copy-start(f32[2,8,8,12]{2,3,1,0:T(8,128)} %copy-done.11) | copy-start | bytes 18436
  121.3 51.9 %copy-start.5 = (bf16[2,8,8,1536]{3,2,1,0:T(8,128)(2,1)S(1)}, bf16[2,8,8,1536]{3,2,1,0:T(8,128)(2,1)}, u32[]{:S(2)}) copy-start(bf16[2,8,8,1536]{3,2,1,0:T(8,128)(2,1)} %param.8) | copy-start | bytes 1179652
  121.3 53.1 %copy-start.2 = (bf16[2,8,8,1536]{3,2,1,0:T(8,128)(2,1)S(1)}, bf16[2,8,8,1536]{3,2,1,0:T(8,128)(2,1)}, u32[]{:S(2)}) copy-start(bf16[2,8,8,1536]{3,2,1,0:T(8,128)(2,1)} %param.9) | copy-start | bytes 1179652
  121.3 11.1 %collective-permute-start.5 = (bf16[2,2,8,8,1536]{4,3,2,1,0:T(8,128)(2,1)S(1)}, bf16[2,2,8,8,1536]{4,3,2,1,0:T(8,128)(2,1)S(1)}, u32[]{:S(2)}, u32[]{:S(2)}) collective-permute-start(bf16[2,2,8,8,1536]{4,3,2,1,0:T(8,128)(2,1)S(1)} %pad_maximum_fusion.5), channel_id=1, source_target_pairs={{2,0},{4,2},{6,4},{3,1},{5,3},{7,5},{10,8},{12,10},{14,12},{11,9},... | collective-permute-start | bytes 2359304 | tf_op jit(solution)/shard_map/ppermute | solution.py:24
  122.7 11.5 %collective-permute-start.4 = (bf16[2,2,8,8,1536]{4,3,2,1,0:T(8,128)(2,1)S(1)}, bf16[2,2,8,8,1536]{4,3,2,1,0:T(8,128)(2,1)S(1)}, u32[]{:S(2)}, u32[]{:S(2)}) collective-permute-start(bf16[2,2,8,8,1536]{4,3,2,1,0:T(8,128)(2,1)S(1)} %pad_maximum_fusion.5), channel_id=1, source_target_pairs={{0,2},{2,4},{4,6},{1,3},{3,5},{5,7},{8,10},{10,12},{12,14},{9,11},... | collective-permute-start | bytes 2359304 | tf_op jit(solution)/shard_map/ppermute | solution.py:22
  135.9 61.0 %collective-permute-start.7 = (bf16[2,2,24,8,1536]{4,3,2,1,0:T(8,128)(2,1)}, bf16[2,2,24,8,1536]{4,3,2,1,0:T(8,128)(2,1)}, u32[]{:S(2)}, u32[]{:S(2)}) collective-permute-start(bf16[2,2,24,8,1536]{4,3,2,1,0:T(8,128)(2,1)} %pad_maximum_fusion.3), channel_id=1, source_target_pairs={{1,0},{3,2},{5,4},{7,6},{9,8},{11,10},{13,12},{15,14},{17,16},{19,... | collective-permute-start | bytes 7077896 | tf_op jit(solution)/shard_map/ppermute | solution.py:24
  137.2 59.7 %collective-permute-start.6 = (bf16[2,2,24,8,1536]{4,3,2,1,0:T(8,128)(2,1)}, bf16[2,2,24,8,1536]{4,3,2,1,0:T(8,128)(2,1)}, u32[]{:S(2)}, u32[]{:S(2)}) collective-permute-start(bf16[2,2,24,8,1536]{4,3,2,1,0:T(8,128)(2,1)} %pad_maximum_fusion.3), channel_id=1, source_target_pairs={{0,1},{2,3},{4,5},{6,7},{8,9},{10,11},{12,13},{14,15},{16,17},{18,... | collective-permute-start | bytes 7077896 | tf_op jit(solution)/shard_map/ppermute | solution.py:22
  146.2 13.8 %collective-permute-start.9 = (f32[2,2,8,8,12]{3,2,1,4,0:T(8,128)}, f32[2,2,8,8,12]{3,2,1,4,0:T(8,128)}, u32[]{:S(2)}, u32[]{:S(2)}) collective-permute-start(f32[2,2,8,8,12]{3,2,1,4,0:T(8,128)} %constant_dynamic-update-slice_fusion), channel_id=1, source_target_pairs={{2,0},{4,2},{6,4},{3,1},{5,3},{7,5},{10,8},{12,10},{14,12},{11,9},... | collective-permute-start | bytes 36872 | tf_op jit(solution)/shard_map/ppermute | solution.py:24
  147.5 14.2 %collective-permute-start.8 = (f32[2,2,8,8,12]{3,2,1,4,0:T(8,128)}, f32[2,2,8,8,12]{3,2,1,4,0:T(8,128)}, u32[]{:S(2)}, u32[]{:S(2)}) collective-permute-start(f32[2,2,8,8,12]{3,2,1,4,0:T(8,128)} %constant_dynamic-update-slice_fusion), channel_id=1, source_target_pairs={{0,2},{2,4},{4,6},{1,3},{3,5},{5,7},{8,10},{10,12},{12,14},{9,11},... | collective-permute-start | bytes 36872 | tf_op jit(solution)/shard_map/ppermute | solution.py:22
  165.3 23.3 %collective-permute-start.11 = (f32[2,2,24,8,12]{2,3,4,1,0:T(8,128)}, f32[2,2,24,8,12]{2,3,4,1,0:T(8,128)}, u32[]{:S(2)}, u32[]{:S(2)}) collective-permute-start(f32[2,2,24,8,12]{2,3,4,1,0:T(8,128)} %pad_maximum_fusion.7), channel_id=1, source_target_pairs={{1,0},{3,2},{5,4},{7,6},{9,8},{11,10},{13,12},{15,14},{17,16},{19,... | collective-permute-start | bytes 110600 | tf_op jit(solution)/shard_map/ppermute | solution.py:24
  166.6 25.2 %collective-permute-start.10 = (f32[2,2,24,8,12]{2,3,4,1,0:T(8,128)}, f32[2,2,24,8,12]{2,3,4,1,0:T(8,128)}, u32[]{:S(2)}, u32[]{:S(2)}) collective-permute-start(f32[2,2,24,8,12]{2,3,4,1,0:T(8,128)} %pad_maximum_fusion.7), channel_id=1, source_target_pairs={{0,1},{2,3},{4,5},{6,7},{8,9},{10,11},{12,13},{14,15},{16,17},{18,... | collective-permute-start | bytes 110600 | tf_op jit(solution)/shard_map/ppermute | solution.py:22
  210.0 4.4 %copy-start.26 = (f32[128]{0:T(128)S(1)}, f32[128]{0:T(128)}, u32[]{:S(2)}) copy-start(f32[128]{0:T(128)} %copy-done.25) | copy-start | bytes 1540
  214.4 5.4 %copy-start = (bf16[2,576,12,128]{3,2,1,0:T(8,128)(2,1)S(1)}, bf16[2,576,12,128]{3,2,1,0:T(8,128)(2,1)}, u32[]{:S(2)}) copy-start(bf16[2,576,12,128]{3,2,1,0:T(8,128)(2,1)} %reshape_squeeze.15) | copy-start | bytes 10616836
  219.8 2.0 copy-start.8
  219.8 2.0 copy-start.18
  219.8 2.5 copy-start.20
  219.8 2.6 copy-start.21
  219.8 2.6 copy-start.23
  219.8 2.6 copy-start.29
  231.3 2.1 copy-start.30
  231.3 48.4 %copy-start.6 = (bf16[2,8,8,1536]{3,2,1,0:T(8,128)(2,1)S(1)}, bf16[2,8,8,1536]{3,2,1,0:T(8,128)(2,1)}, u32[]{:S(2)}) copy-start(bf16[2,8,8,1536]{3,2,1,0:T(8,128)(2,1)} %param.8) | copy-start | bytes 1179652
  231.3 48.4 %copy-start.13 = (f32[2,8,8,12]{2,3,1,0:T(8,128)S(1)}, f32[2,8,8,12]{2,3,1,0:T(8,128)}, u32[]{:S(2)}) copy-start(f32[2,8,8,12]{2,3,1,0:T(8,128)} %copy-done.11) | copy-start | bytes 18436
where the time goes:
time: 283 us; the launch traced here: 281 us
  blocking collectives  59.1 us (21%)
  local copies, waits for them, and re-layouts  56 us (20%)
  waiting for transfers between devices  55.1 us (19%)
  starting transfers between devices  52.9 us (19%)
  matrix products  33.4 us (12%)
  other arithmetic  22.4 us (8%)
    psum x1, blocking collectives, body(): whole_sum = lax.psum(gain_parts, ('fsdp', 'ty', 'tx'))  45.7 us
    ppermute x6, waiting for transfers between devices, padded(): lax.ppermute(head, axis, [((i + 1) % count, i) for i in range(ends)])  45 us
    ppermute x6, starting transfers between devices, padded(): lax.ppermute(tail, axis, [(i, (i + 1) % count) for i in range(ends)])  44.9 us
    dot_general x6, matrix products, product(): return jnp.einsum(form, left, right, preferred_element_type=jnp.float32)  33.4 us
    another operation x4, local copies, waits for them, and re-layouts, as_near(): return field.reshape(frame_count, near_rows, head_count, head_size)  23.6 us
    concatenate x6, other arithmetic, padded(): jnp.concatenate([lax.ppermute(tail, axis, [(i, (i + 1) % count) for i in...  14.2 us
    unnamed x1, blocking collectives  13.4 us
    ppermute x6, waiting for transfers between devices, padded(): lax.ppermute(tail, axis, [(i, (i + 1) % count) for i in range(ends)])  10 us
  transfers between devices with their start and end apart: 12, of which 6 were waited for; matrix products, arithmetic and copies ran while one was open for 9% of the time, Pallas kernels for 0%

commit v1 on v0

v1 whole, which is shorter than its diff:
```python
import functools
import math

import jax
import jax.numpy as jnp
from jax import lax
from jax.experimental import pallas as pl
from jax.experimental.pallas import tpu as pltpu
from jax.sharding import PartitionSpec as P

TILE = 8
NORM_EPS = 1e-06
CLOSED = -1e30
MESH = pl.DeviceIdType.MESH
V, K, D, Q = 0, 1, 2, 3
UNROLL = 2


def dot_nt(left, right):
    return lax.dot_general(
        left, right, (((1,), (1,)), ((), ())), preferred_element_type=jnp.float32
    )


def dot_nn(left, right):
    return lax.dot_general(
        left, right, (((1,), (0,)), ((), ())), preferred_element_type=jnp.float32
    )


def norm_parts(raw):
    floats = raw.astype(jnp.float32)
    inverse = lax.rsqrt(jnp.mean(floats * floats, axis=-1, keepdims=True) + NORM_EPS)
    return floats * inverse, inverse


def when(cond, act):
    if cond is None:
        act()
    else:
        pl.when(cond)(act)


def both(one, two):
    if one is None:
        return two
    if two is None:
        return one
    return jnp.logical_and(one, two)


def kernel(
    dims,
    win_ref,
    gain_ref,
    q_ref,
    k_ref,
    v_ref,
    d_ref,
    out_ref,
    qg_ref,
    kg_ref,
    vg_ref,
    part_ref,
    near,
    stat,
    srow,
    bias,
    gains,
    gain_send,
    gain_recv,
    x_send,
    x_recv,
    ty_send,
    ty_recv,
):
    fsdp, ty, tx, frames, rows, heads, size, slots = dims
    width = heads * size
    z = lax.axis_index("fsdp")
    t = lax.axis_index("ty")
    x = lax.axis_index("tx")
    scale = 1.0 / math.sqrt(size)
    exp_scale = scale * math.log2(math.e)

    if tx == 1:
        x_links = []
    elif tx == 2:
        x_links = [(1, 1 - x, None, None)]
    else:
        x_links = [(1, x + 1, x < tx - 1, x > 0), (2, x - 1, x > 0, x < tx - 1)]
    ty_links = [(1, t + 1, t < ty - 1, t > 0), (2, t - 1, t > 0, t < ty - 1)]

    barrier = pltpu.get_barrier_semaphore()

    def greet(cond, device):
        when(cond, lambda: pl.semaphore_signal(
            barrier, inc=1, device_id=device, device_id_type=MESH))

    for step in range(1, fsdp):
        greet(None, {"fsdp": lax.rem(z + step, fsdp)})
    for _, peer, sends, _ in x_links:
        greet(sends, {"tx": peer})
    for _, peer, sends, _ in ty_links:
        greet(sends, {"ty": peer})

    def block(buffer, chunk, slot):
        if buffer is stat:
            return stat.at[chunk, slot]
        array, frame = chunk
        return near.at[array, frame, pl.ds(slot * rows, rows)]

    def sem_index(buffer, chunk):
        if buffer is stat:
            return 4 * frames + chunk
        return chunk[0] * frames + chunk[1]

    def x_copy(link, buffer, chunk):
        column, peer, _, _ = link
        s = sem_index(buffer, chunk)
        return pltpu.make_async_remote_copy(
            src_ref=block(buffer, chunk, 0),
            dst_ref=block(buffer, chunk, 3 * column),
            send_sem=x_send.at[column - 1, s],
            recv_sem=x_recv.at[column - 1, s],
            device_id={"tx": peer},
            device_id_type=MESH,
        )

    def ty_copy(link, column, buffer, chunk):
        row, peer, _, _ = link
        s = sem_index(buffer, chunk)
        return pltpu.make_async_remote_copy(
            src_ref=block(buffer, chunk, 3 * column),
            dst_ref=block(buffer, chunk, 3 * column + row),
            send_sem=ty_send.at[row - 1, column, s],
            recv_sem=ty_recv.at[row - 1, column, s],
            device_id={"ty": peer},
            device_id_type=MESH,
        )

    def start_x(buffer, chunk):
        for link in x_links:
            when(link[2], lambda link=link: x_copy(link, buffer, chunk).start())

    def start_ty(buffer, chunk):
        for link in ty_links:
            when(link[2], lambda link=link: ty_copy(link, 0, buffer, chunk).start())

    def forward(buffer, chunk):
        for x_link in x_links:
            when(x_link[3], lambda x_link=x_link: x_copy(x_link, buffer, chunk).wait_recv())
            for link in ty_links:
                when(
                    both(link[2], x_link[3]),
                    lambda link=link, x_link=x_link: ty_copy(
                        link, x_link[0], buffer, chunk).start(),
                )

    def arrive(buffer, chunk):
        for link in ty_links:
            when(link[3], lambda link=link: ty_copy(link, 0, buffer, chunk).wait_recv())
            for x_link in x_links:
                when(
                    both(link[3], x_link[3]),
                    lambda link=link, x_link=x_link: ty_copy(
                        link, x_link[0], buffer, chunk).wait_recv(),
                )

    def finish(buffer, chunk):
        for link in x_links:
            when(link[2], lambda link=link: x_copy(link, buffer, chunk).wait_send())
        for link in ty_links:
            when(link[2], lambda link=link: ty_copy(link, 0, buffer, chunk).wait_send())
            for x_link in x_links:
                when(
                    both(link[2], x_link[3]),
                    lambda link=link, x_link=x_link: ty_copy(
                        link, x_link[0], buffer, chunk).wait_send(),
                )

    def clear(slot):
        near[:, :, slot * rows:(slot + 1) * rows, :] = jnp.zeros(
            (4, frames, rows, width), near.dtype)
        stat[:, slot] = jnp.zeros((frames,) + stat.shape[2:], stat.dtype)

    exists = [None] * slots
    for column in range(slots // 3):
        have_column = None
        for link in x_links:
            if link[0] == column:
                have_column = link[3]
        exists[3 * column] = have_column
        for link in ty_links:
            exists[3 * column + link[0]] = both(link[3], have_column)
    for slot in range(slots):
        if slot >= 3 * (slots // 3):
            exists[slot] = False
            clear(slot)
        elif exists[slot] is not None:
            pl.when(jnp.logical_not(exists[slot]))(functools.partial(clear, slot))

    lane = lax.broadcasted_iota(jnp.int32, (1, 2 * rows), 1)
    for head in range(heads):
        row_bias = jnp.where(win_ref[head, 0] >= 3, 0.0, CLOSED)
        col_bias = jnp.where(win_ref[head, 1] >= 3, 0.0, CLOSED)
        terms = []
        for slot in range(slots):
            term = jnp.float32(0.0)
            if slot % 3 != 0:
                term = term + row_bias
            if slot // 3 != 0:
                term = term + col_bias
            if exists[slot] is False:
                term = jnp.float32(CLOSED)
            elif exists[slot] is not None:
                term = term + jnp.where(exists[slot], 0.0, CLOSED)
            terms.append(term)
        for pair in range(slots // 2):
            bias[head:head + 1, pair * 2 * rows:(pair + 1) * 2 * rows] = jnp.where(
                lane < rows, terms[2 * pair], terms[2 * pair + 1])

    for frame in range(frames):
        span = slice(frame * rows, (frame + 1) * rows)
        near[V, frame, 0:rows, :] = v_ref[span, :]
        near[D, frame, 0:rows, :] = d_ref[span, :]
    gains[pl.ds(z, 1)] = gain_ref[...][None]

    greeted = fsdp - 1
    for _, _, _, receives in x_links + ty_links:
        greeted = greeted + (1 if receives is None else receives.astype(jnp.int32))
    pl.semaphore_wait(barrier, greeted)

    def gain_copy(step):
        return pltpu.make_async_remote_copy(
            src_ref=gain_ref,
            dst_ref=gains.at[z],
            send_sem=gain_send.at[step - 1],
            recv_sem=gain_recv.at[step - 1],
            device_id={"fsdp": lax.rem(z + step, fsdp)},
            device_id_type=MESH,
        )

    for step in range(1, fsdp):
        gain_copy(step).start()
    start_x(near, (V, 0))
    start_ty(near, (V, 0))
    for step in range(1, fsdp):
        gain_copy(step).wait()
    gain_all = jnp.sum(gains[...], axis=0)
    q_gain = gain_all[0:1]
    k_gain = gain_all[1:2]

    def place(source, array, frame, gain):
        def one(head, carry):
            cols = pl.ds(pl.multiple_of(head * size, size), size)
            normed, _ = norm_parts(source[frame * rows:(frame + 1) * rows, cols])
            near[array, frame, 0:rows, cols] = (normed * gain).astype(near.dtype)
            return carry

        lax.fori_loop(0, heads, one, 0)

    place(k_ref, K, 0, k_gain)
    start_x(near, (K, 0))
    start_ty(near, (K, 0))
    for frame in range(1, frames):
        start_x(near, (V, frame))
        place(k_ref, K, frame, k_gain)
        start_x(near, (K, frame))
    for frame in range(frames):
        start_x(near, (D, frame))
        place(q_ref, Q, frame, q_gain)
        start_x(near, (Q, frame))

    stat_lane = lax.broadcasted_iota(jnp.int32, (rows, stat.shape[3]), 1)

    def backward(raw, upstream, gain):
        normed, inverse = norm_parts(raw)
        part = jnp.sum(upstream * normed, axis=0, keepdims=True)
        scaled = upstream * gain
        mean = jnp.mean(scaled * normed, axis=-1, keepdims=True)
        return inverse * (scaled - normed * mean), part

    def query_head(frame, head, held, part):
        cols = pl.ds(pl.multiple_of(head * size, size), size)
        span = slice(frame * rows, (frame + 1) * rows)
        keys = near[K, frame, :, cols]
        vals = near[V, frame, :, cols]
        queries = near[Q, frame, 0:rows, cols]
        grads = near[D, frame, 0:rows, cols]
        weights = jnp.exp2(dot_nt(queries, keys) * exp_scale + bias[pl.ds(head, 1), :])
        inverse = 1.0 / jnp.sum(weights, axis=-1, keepdims=True)
        shares = weights * inverse
        output = dot_nn(shares.astype(jnp.bfloat16), vals).astype(jnp.bfloat16)
        out_ref[span, cols] = output
        delta = jnp.sum(
            grads.astype(jnp.float32) * output.astype(jnp.float32), axis=-1, keepdims=True)
        share_grad = dot_nt(grads, vals)
        score_grad = (shares * (share_grad - delta)).astype(jnp.bfloat16)
        raw_grad, more = backward(
            q_ref[span, cols], dot_nn(score_grad, keys) * scale, q_gain)
        qg_ref[span, cols] = raw_grad.astype(jnp.bfloat16)
        held = jnp.where(stat_lane == head, inverse, held)
        held = jnp.where(stat_lane == 16 + head, delta, held)
        return held, part + more

    def query_side(frame, part):
        def some(step, carry):
            held, part = carry
            for k in range(UNROLL):
                held, part = query_head(frame, step * UNROLL + k, held, part)
            return held, part

        held, part = lax.fori_loop(
            0, heads // UNROLL, some,
            (jnp.zeros((rows, stat.shape[3]), jnp.float32), part))
        turned = jnp.transpose(jnp.concatenate([held, held], axis=0))
        stat[frame, 0] = turned[0:stat.shape[2]]
        return part

    def key_head(frame, head, part):
        cols = pl.ds(pl.multiple_of(head * size, size), size)
        span = slice(frame * rows, (frame + 1) * rows)
        keys = near[K, frame, 0:rows, cols]
        vals = near[V, frame, 0:rows, cols]
        queries = near[Q, frame, :, cols]
        grads = near[D, frame, :, cols]
        weights = jnp.exp2(dot_nt(keys, queries) * exp_scale + bias[pl.ds(head, 1), :])
        shares = weights * srow[pl.ds(head, 1), :]
        vg_ref[span, cols] = dot_nn(shares.astype(jnp.bfloat16), grads).astype(jnp.bfloat16)
        share_grad = dot_nt(vals, grads)
        score_grad = (shares * (share_grad - srow[pl.ds(16 + head, 1), :])).astype(jnp.bfloat16)
        raw_grad, more = backward(
            k_ref[span, cols], dot_nn(score_grad, queries) * scale, k_gain)
        kg_ref[span, cols] = raw_grad.astype(jnp.bfloat16)
        return part + more

    def key_side(frame, part):
        side = lax.broadcasted_iota(jnp.int32, (stat.shape[2], 2 * rows), 1)
        for pair in range(slots // 2):
            srow[:, pair * 2 * rows:(pair + 1) * 2 * rows] = jnp.where(
                side < rows, stat[frame, 2 * pair], stat[frame, 2 * pair + 1])

        def some(step, part):
            for k in range(UNROLL):
                part = key_head(frame, step * UNROLL + k, part)
            return part

        return lax.fori_loop(0, heads // UNROLL, some, part)

    pairs = [(V, K, frame) for frame in range(frames)]
    pairs += [(D, Q, frame) for frame in range(frames)]
    part = jnp.zeros((1, size), jnp.float32)
    for place_in, (first, second, frame) in enumerate(pairs):
        forward(near, (first, frame))
        forward(near, (second, frame))
        if place_in + 1 < len(pairs):
            later = pairs[place_in + 1]
            start_ty(near, (later[0], later[2]))
            start_ty(near, (later[1], later[2]))
        if first == D:
            forward(stat, frame)
        arrive(near, (first, frame))
        arrive(near, (second, frame))
        if first == V:
            part = query_side(frame, part)
            start_x(stat, frame)
            start_ty(stat, frame)
            if frame == frames - 1:
                part_ref[0:1, :] = part
                part = jnp.zeros((1, size), jnp.float32)
        else:
            arrive(stat, frame)
            part = key_side(frame, part)
    part_ref[1:2, :] = part
    part_ref[2:8, :] = jnp.zeros((6, size), jnp.float32)

    for frame in range(frames):
        for array in range(4):
            finish(near, (array, frame))
        finish(stat, frame)


def body(axes, q_raw, k_raw, values, d_out, q_gain, k_gain, windows):
    fsdp, ty, tx = axes
    frames, height, across, width = q_raw.shape
    rows = height * across
    heads = windows.shape[0]
    size = width // heads
    columns = min(tx, 3)
    slots = 3 * columns + (3 * columns) % 2
    share = q_gain.shape[0]
    mine = jnp.arange(size, dtype=jnp.int32) // share == lax.axis_index("fsdp")
    placed = jnp.where(
        mine[None, :], jnp.stack([jnp.tile(q_gain, fsdp), jnp.tile(k_gain, fsdp)]), 0.0)
    placed = jnp.pad(placed, ((0, 6), (0, 0)))

    flat = (frames * rows, width)
    field = jax.ShapeDtypeStruct(flat, jnp.bfloat16)
    vmem = pl.BlockSpec(memory_space=pltpu.VMEM)
    sems = 5 * frames
    dims = (fsdp, ty, tx, frames, rows, heads, size, slots)
    dma = pltpu.SemaphoreType.DMA
    side = max(columns - 1, 1)
    output, q_grad, k_grad, v_grad, parts = pl.pallas_call(
        functools.partial(kernel, dims),
        out_shape=[field] * 4 + [jax.ShapeDtypeStruct((8, size), jnp.float32)],
        in_specs=[pl.BlockSpec(memory_space=pltpu.SMEM)] + [vmem] * 5,
        out_specs=[vmem] * 5,
        scratch_shapes=[
            pltpu.VMEM((4, frames, slots * rows, width), jnp.bfloat16),
            pltpu.VMEM((frames, slots, 32, 2 * rows), jnp.float32),
            pltpu.VMEM((32, slots * rows), jnp.float32),
            pltpu.VMEM((16, slots * rows), jnp.float32),
            pltpu.VMEM((fsdp, 8, size), jnp.float32),
            dma((max(fsdp - 1, 1),)),
            dma((max(fsdp - 1, 1),)),
            dma((side, sems)),
            dma((side, sems)),
            dma((2, columns, sems)),
            dma((2, columns, sems)),
        ],
        compiler_params=pltpu.CompilerParams(
            collective_id=0, has_side_effects=True, vmem_limit_bytes=48 * 1024 * 1024),
    )(
        windows,
        placed,
        q_raw.reshape(flat),
        k_raw.reshape(flat),
        values.reshape(flat),
        d_out.reshape(flat),
    )
    whole_sum = lax.psum(parts[0:2], ("fsdp", "ty", "tx"))
    owned = lax.dynamic_slice_in_dim(whole_sum, lax.axis_index("fsdp") * share, share, 1)
    return (
        output.reshape(q_raw.shape),
        q_grad.reshape(q_raw.shape),
        k_grad.reshape(q_raw.shape),
        v_grad.reshape(q_raw.shape),
        owned[0],
        owned[1],
    )


def solution(mesh):
    axes = tuple(mesh.shape[name] for name in ("fsdp", "ty", "tx"))
    spec = P("fsdp", "ty", "tx", None)
    return jax.shard_map(
        functools.partial(body, axes),
        mesh=mesh,
        in_specs=(spec, spec, spec, spec, P("fsdp"), P("fsdp"), P()),
        out_specs=(spec, spec, spec, spec, P("fsdp"), P("fsdp")),
        check_vma=False,
    )
```

time: 283 us -> 120 us (0.42)
  Pallas kernels: 0 us -> 66.7 us
  waiting for transfers between devices: 55.1 us -> 0 us
  starting transfers between devices: 52.9 us -> 0 us
  local copies, waits for them, and re-layouts: 56 us -> 9.7 us
  matrix products: 33.4 us -> 0 us
  other arithmetic: 22.4 us -> 0.02 us
  blocking collectives: 59.1 us -> 43 us
    pallas_call x0 -> x1, Pallas kernels: none -> 66.7 us  [body(): pl.pallas_call(functools.partial(kernel, dims), out_shape=[field] * 4 + [...]
    ppermute x12 -> x0, waiting for transfers between devices: 55.1 us -> none  [the longest x6 45 us: padded(): lax.ppermute(head, axis, [((i + 1) % count, i) for i in range(ends)])]
    ppermute x12 -> x0, starting transfers between devices: 52.9 us -> none  [the longest x6 44.9 us: padded(): lax.ppermute(tail, axis, [(i, (i + 1) % count) for i in range(ends)])]
    dot_general x6 -> x0, matrix products: 33.4 us -> none  [product(): return jnp.einsum(form, left, right, preferred_element_type=jnp.float32)]
    another operation x8 -> x4, local copies, waits for them, and re-layouts: 25.4 us -> 0.17 us  [the longest x2 0.17 us: body(): jnp.stack([jnp.tile(q_gain, fsdp), jnp.tile(k_gain, fsdp)])]
    concatenate x6 -> x0, other arithmetic: 14.2 us -> none  [padded(): jnp.concatenate([lax.ppermute(tail, axis, [(i, (i + 1) % count) for i in...]
    unnamed x1 -> x0, blocking collectives: 13.4 us -> none
    slice x5 -> x1, local copies, waits for them, and re-layouts: 6.9 us -> 0.01 us  [body(): whole_sum = lax.psum(parts[0:2], ('fsdp', 'ty', 'tx'))]
  transfers between devices with their start and end apart: 12 -> 0, of which waited for: 6 -> 0; matrix products, arithmetic and copies ran while one was open for 9% -> 0% of each run, Pallas kernels for 0% -> 0%
where the time goes in v1:
time: 120 us
  Pallas kernels  66.7 us (56%)
  blocking collectives  43 us (36%)
  local copies, waits for them, and re-layouts  9.7 us (8%)
    pallas_call x1, Pallas kernels, body(): pl.pallas_call(functools.partial(kernel, dims), out_shape=[field] * 4 + [...  66.7 us
    psum x1, blocking collectives, body(): whole_sum = lax.psum(parts[0:2], ('fsdp', 'ty', 'tx'))  43 us
    unnamed x19, local copies, waits for them, and re-layouts  8.92 us

profile of v1, /device:TPU:0, one launch (start us, length us, event | category | flops | bytes accessed | tf_op | source)
XLA Modules:
  0.0 120.1 jit_solution(13587036261478843318)
XLA Ops:
  0.6 0.0 copy-start.5
  0.7 0.6 copy-done.5
  1.3 0.0 copy-start.6
  1.3 0.1 stack_tile.6
  1.4 0.6 copy-done.6
  2.0 0.1 stack_tile.7
  2.1 0.0 copy-start.4
  2.1 0.7 copy-done.4
  2.7 0.1 copy.13.win_ref
  2.8 0.0 copy-start
  2.8 1.0 copy-done
  3.8 0.0 copy-start.1
  3.8 1.0 copy-done.1
  4.8 0.0 copy-start.2
  4.8 1.0 copy-done.2
  5.8 0.0 copy-start.3
  5.8 1.0 copy-done.3
  6.8 66.7 %shard_map.118 = (bf16[128,1536]{1,0:T(8,128)(2,1)S(1)}, bf16[128,1536]{1,0:T(8,128)(2,1)S(1)}, bf16[128,1536]{1,0:T(8,128)(2,1)S(1)}, bf16[128,1536]{1,0:T(8,128)(2,1)S(1)}, f32[8,128]{1,0:T(8,128)S(1)}) custom-call(s32[12,2]{1,0:T(8,128)S(1)} %copy.13.win_ref, f32[8,128]{1,0:T(8,128)S(1)} %pad.4.gain_ref, bf16[128,1536]{1,0:T(8,128)(2,1)S(1)} %bitcast.16, ...), custom_call_target="tpu_custom_call" | custom-call | tf_op jit(solution)/shard_map/pallas_call | solution.py:404
  73.5 43.0 %psum.7 = f32[2,128]{1,0:T(2,128)S(1)} all-reduce(f32[2,128]{1,0:T(2,128)S(1)} %slice.9), channel_id=1, replica_groups=mesh['fsdp'=4,'ty'=4,'tx'=2] {'fsdp','ty','tx'}, use_global_device_ids=true, to_apply=%region_0.1 | all-reduce | flops 256 | bytes 2048 | tf_op jit(solution)/shard_map/psum | solution.py:432
  116.5 0.1 constant_dynamic-slice_fusion
  116.6 0.5 slice_bitcast_fusion
  117.1 0.7 copy.18
  117.9 0.7 copy.19
  118.6 0.7 copy.20
  119.4 0.7 copy.21
  (6 shorter events, 0.0 us)
Async XLA Ops:
  0.6 0.7 copy-start.5
  1.3 0.7 copy-start.6
  2.1 0.7 copy-start.4
  2.8 1.0 copy-start
  3.8 1.0 copy-start.1
  4.8 1.0 copy-start.2
  5.8 1.0 copy-start.3

commit v2 on v1

--- a/solution.py
+++ b/solution.py
@@ -13,7 +13,7 @@
 CLOSED = -1e30
 MESH = pl.DeviceIdType.MESH
 V, K, D, Q = 0, 1, 2, 3
-UNROLL = 2
+UNROLL = 4
 
 
 def dot_nt(left, right):
@@ -52,23 +52,31 @@
 def kernel(
     dims,
     win_ref,
-    gain_ref,
-    q_ref,
-    k_ref,
-    v_ref,
-    d_ref,
+    q_gain_ref,
+    k_gain_ref,
+    q_hbm,
+    k_hbm,
+    v_hbm,
+    d_hbm,
     out_ref,
     qg_ref,
     kg_ref,
     vg_ref,
-    part_ref,
+    q_part_ref,
+    k_part_ref,
     near,
     stat,
     srow,
     bias,
     gains,
+    q_ref,
+    k_ref,
+    sums,
+    load_sem,
     gain_send,
     gain_recv,
+    sum_send,
+    sum_recv,
     x_send,
     x_recv,
     ty_send,
@@ -92,16 +100,24 @@
 
     barrier = pltpu.get_barrier_semaphore()
 
-    def greet(cond, device):
-        when(cond, lambda: pl.semaphore_signal(
-            barrier, inc=1, device_id=device, device_id_type=MESH))
-
-    for step in range(1, fsdp):
-        greet(None, {"fsdp": lax.rem(z + step, fsdp)})
-    for _, peer, sends, _ in x_links:
-        greet(sends, {"tx": peer})
-    for _, peer, sends, _ in ty_links:
-        greet(sends, {"ty": peer})
+    def greet(device):
+        pl.semaphore_signal(barrier, inc=1, device_id=device, device_id_type=MESH)
+
+    lines = (("fsdp", z, fsdp), ("tx", x, tx), ("ty", t, ty))
+    for axis, place_in, count in lines:
+        for step in range(1, count):
+            greet({axis: lax.rem(place_in + step, count)})
+
+    loads = [
+        pltpu.make_async_copy(source.at[frame * rows:(frame + 1) * rows], target, load_sem.at[i])
+        for i, (source, frame, target) in enumerate(
+            [(v_hbm, frame, near.at[V, frame, 0:rows]) for frame in range(frames)]
+            + [(k_hbm, frame, k_ref.at[frame * rows:(frame + 1) * rows]) for frame in range(frames)]
+            + [(d_hbm, frame, near.at[D, frame, 0:rows]) for frame in range(frames)]
+            + [(q_hbm, frame, q_ref.at[frame * rows:(frame + 1) * rows]) for frame in range(frames)])
+    ]
+    for load in loads:
+        load.start()
 
     def block(buffer, chunk, slot):
         if buffer is stat:
@@ -201,8 +217,8 @@
 
     lane = lax.broadcasted_iota(jnp.int32, (1, 2 * rows), 1)
     for head in range(heads):
-        row_bias = jnp.where(win_ref[head, 0] >= 3, 0.0, CLOSED)
-        col_bias = jnp.where(win_ref[head, 1] >= 3, 0.0, CLOSED)
+        row_bias = jnp.where(win_ref[0, head] >= 3, 0.0, CLOSED)
+        col_bias = jnp.where(win_ref[1, head] >= 3, 0.0, CLOSED)
         terms = []
         for slot in range(slots):
             term = jnp.float32(0.0)
@@ -219,20 +235,17 @@
             bias[head:head + 1, pair * 2 * rows:(pair + 1) * 2 * rows] = jnp.where(
                 lane < rows, terms[2 * pair], terms[2 * pair + 1])
 
-    for frame in range(frames):
-        span = slice(frame * rows, (frame + 1) * rows)
-        near[V, frame, 0:rows, :] = v_ref[span, :]
-        near[D, frame, 0:rows, :] = d_ref[span, :]
-    gains[pl.ds(z, 1)] = gain_ref[...][None]
-
-    greeted = fsdp - 1
-    for _, _, _, receives in x_links + ty_links:
-        greeted = greeted + (1 if receives is None else receives.astype(jnp.int32))
-    pl.semaphore_wait(barrier, greeted)
+    share = size // fsdp
+    gains[z] = jnp.zeros((8, size), jnp.float32)
+    gains[z, 0:1, 0:share] = q_gain_ref[...]
+    gains[z, 1:2, 0:share] = k_gain_ref[...]
+    gains[z] = pltpu.roll(gains[z], z * share, 1)
+
+    pl.semaphore_wait(barrier, fsdp + tx + ty - 3)
 
     def gain_copy(step):
         return pltpu.make_async_remote_copy(
-            src_ref=gain_ref,
+            src_ref=gains.at[z],
             dst_ref=gains.at[z],
             send_sem=gain_send.at[step - 1],
             recv_sem=gain_recv.at[step - 1],
@@ -242,8 +255,11 @@
 
     for step in range(1, fsdp):
         gain_copy(step).start()
+    loads[0].wait()
     start_x(near, (V, 0))
     start_ty(near, (V, 0))
+    for load in loads[1:]:
+        load.wait()
     for step in range(1, fsdp):
         gain_copy(step).wait()
     gain_all = jnp.sum(gains[...], axis=0)
@@ -366,18 +382,52 @@
             start_x(stat, frame)
             start_ty(stat, frame)
             if frame == frames - 1:
-                part_ref[0:1, :] = part
+                q_part = part
                 part = jnp.zeros((1, size), jnp.float32)
         else:
             arrive(stat, frame)
             part = key_side(frame, part)
-    part_ref[1:2, :] = part
-    part_ref[2:8, :] = jnp.zeros((6, size), jnp.float32)
+    side = lax.broadcasted_iota(jnp.int32, (8, size), 0)
+    total = jnp.where(side == 0, q_part, jnp.where(side == 1, part, 0.0))
+    first = 0
+    for axis, place_in, count in lines:
+        if count > 1:
+            sums[first + place_in] = total
+
+            def sum_copy(step, axis=axis, place_in=place_in, count=count, first=first):
+                return pltpu.make_async_remote_copy(
+                    src_ref=sums.at[first + place_in],
+                    dst_ref=sums.at[first + place_in],
+                    send_sem=sum_send.at[first + step],
+                    recv_sem=sum_recv.at[first + step],
+                    device_id={axis: lax.rem(place_in + step, count)},
+                    device_id_type=MESH,
+                )
+
+            for step in range(1, count):
+                sum_copy(step).start()
+            for step in range(1, count):
+                sum_copy(step).wait()
+            total = jnp.sum(sums[first:first + count], axis=0)
+        first += count
+    owned = pltpu.roll(total, lax.rem(size - z * share, size), 1)
+    q_part_ref[...] = owned[0:1, 0:share]
+    k_part_ref[...] = owned[1:2, 0:share]
 
     for frame in range(frames):
         for array in range(4):
             finish(near, (array, frame))
         finish(stat, frame)
+
+
+def store(*refs):
+    copies = [
+        pltpu.make_async_copy(refs[i], refs[4 + i], refs[8].at[i]) for i in range(4)
+    ]
+    for copy in copies:
+        copy.start()
+    for copy in copies:
+        copy.wait()
 
 
 def body(axes, q_raw, k_raw, values, d_out, q_gain, k_gain, windows):
@@ -389,11 +439,6 @@
     columns = min(tx, 3)
     slots = 3 * columns + (3 * columns) % 2
     share = q_gain.shape[0]
-    mine = jnp.arange(size, dtype=jnp.int32) // share == lax.axis_index("fsdp")
-    placed = jnp.where(
-        mine[None, :], jnp.stack([jnp.tile(q_gain, fsdp), jnp.tile(k_gain, fsdp)]), 0.0)
-    placed = jnp.pad(placed, ((0, 6), (0, 0)))
-
     flat = (frames * rows, width)
     field = jax.ShapeDtypeStruct(flat, jnp.bfloat16)
     vmem = pl.BlockSpec(memory_space=pltpu.VMEM)
@@ -401,44 +446,52 @@
     dims = (fsdp, ty, tx, frames, rows, heads, size, slots)
     dma = pltpu.SemaphoreType.DMA
     side = max(columns - 1, 1)
-    output, q_grad, k_grad, v_grad, parts = pl.pallas_call(
+    hbm = pl.BlockSpec(memory_space=pltpu.HBM)
+    gain_field = jax.ShapeDtypeStruct((1, share), jnp.float32)
+    peers = fsdp + ty + tx
+    *fields, q_part, k_part = pl.pallas_call(
         functools.partial(kernel, dims),
-        out_shape=[field] * 4 + [jax.ShapeDtypeStruct((8, size), jnp.float32)],
-        in_specs=[pl.BlockSpec(memory_space=pltpu.SMEM)] + [vmem] * 5,
-        out_specs=[vmem] * 5,
+        out_shape=[field] * 4 + [gain_field] * 2,
+        in_specs=[pl.BlockSpec(memory_space=pltpu.SMEM)] + [vmem] * 2 + [hbm] * 4,
+        out_specs=[vmem] * 6,
         scratch_shapes=[
             pltpu.VMEM((4, frames, slots * rows, width), jnp.bfloat16),
             pltpu.VMEM((frames, slots, 32, 2 * rows), jnp.float32),
             pltpu.VMEM((32, slots * rows), jnp.float32),
             pltpu.VMEM((16, slots * rows), jnp.float32),
             pltpu.VMEM((fsdp, 8, size), jnp.float32),
+            pltpu.VMEM(flat, jnp.bfloat16),
+            pltpu.VMEM(flat, jnp.bfloat16),
+            pltpu.VMEM((peers, 8, size), jnp.float32),
+            dma((4 * frames,)),
             dma((max(fsdp - 1, 1),)),
             dma((max(fsdp - 1, 1),)),
+            dma((peers,)),
+            dma((peers,)),
             dma((side, sems)),
             dma((side, sems)),
             dma((2, columns, sems)),
             dma((2, columns, sems)),
         ],
         compiler_params=pltpu.CompilerParams(
-            collective_id=0, has_side_effects=True, vmem_limit_bytes=48 * 1024 * 1024),
+            collective_id=0, has_side_effects=True, vmem_limit_bytes=65400 * 1024),
     )(
-        windows,
-        placed,
+        windows.T,
+        q_gain.reshape(1, share),
+        k_gain.reshape(1, share),
         q_raw.reshape(flat),
         k_raw.reshape(flat),
         values.reshape(flat),
         d_out.reshape(flat),
     )
-    whole_sum = lax.psum(parts[0:2], ("fsdp", "ty", "tx"))
-    owned = lax.dynamic_slice_in_dim(whole_sum, lax.axis_index("fsdp") * share, share, 1)
-    return (
-        output.reshape(q_raw.shape),
-        q_grad.reshape(q_raw.shape),
-        k_grad.reshape(q_raw.shape),
-        v_grad.reshape(q_raw.shape),
-        owned[0],
-        owned[1],
-    )
+    fields = pl.pallas_call(
+        store,
+        out_shape=[field] * 4,
+        in_specs=[pl.BlockSpec(memory_space=pl.ANY)] * 4,
+        out_specs=[hbm] * 4,
+        scratch_shapes=[dma((4,))],
+    )(*fields)
+    return tuple(one.reshape(q_raw.shape) for one in fields) + (q_part[0], k_part[0])
 
 
 def solution(mesh):

time: 120 us -> 131 us (1.092)
  Pallas kernels: 66.7 us -> 128 us
  blocking collectives: 43 us -> 0 us
  local copies, waits for them, and re-layouts: 9.7 us -> 1.76 us
    pallas_call x0 -> x1, Pallas kernels: none -> 48.8 us  [body(): pl.pallas_call(store, out_shape=[field] * 4, in_specs=[pl.BlockSpec(memor...]
    psum x1 -> x0, blocking collectives: 43 us -> none  [body(): whole_sum = lax.psum(parts[0:2], ('fsdp', 'ty', 'tx'))]
    pallas_call x1, Pallas kernels: 66.7 us -> 79.3 us  [body(): pl.pallas_call(functools.partial(kernel, dims), out_shape=[field] * 4 + [...]
    unnamed x19 -> x6, local copies, waits for them, and re-layouts: 8.92 us -> 1.76 us
where the time goes in v2:
time: 131 us
  Pallas kernels  128 us (98%)
  local copies, waits for them, and re-layouts  1.76 us (1%)
    pallas_call x1, Pallas kernels, body(): pl.pallas_call(functools.partial(kernel, dims), out_shape=[field] * 4 + [...  79.3 us
    pallas_call x1, Pallas kernels, body(): pl.pallas_call(store, out_shape=[field] * 4, in_specs=[pl.BlockSpec(memor...  48.8 us

profile of v2, /device:TPU:0, one launch (start us, length us, event | category | flops | bytes accessed | tf_op | source)
XLA Modules:
  0.0 130.5 jit_solution(625800663954114619)
XLA Ops:
  0.6 79.3 %shard_map.118 = (bf16[128,1536]{1,0:T(8,128)(2,1)}, bf16[128,1536]{1,0:T(8,128)(2,1)}, bf16[128,1536]{1,0:T(8,128)(2,1)}, bf16[128,1536]{1,0:T(8,128)(2,1)}, f32[1,32]{1,0:T(1,128)}, /*index=5*/f32[1,32]{1,0:T(1,128)}) custom-call(s32[2,12]{1,0:T(2,128)} %bitcast.17, f32[1,32]{1,0:T(1,128)} %bitcast.18, f32[1,32]{1,0:T(1,128)} %bitcast.19, ...), custom_call_target="tpu_custom_call" | custom-call | tf_op jit(solution)/shard_map/pallas_call | solution.py:452
  80.0 48.8 %shard_map.119 = (bf16[128,1536]{1,0:T(8,128)(2,1)}, bf16[128,1536]{1,0:T(8,128)(2,1)}, bf16[128,1536]{1,0:T(8,128)(2,1)}, bf16[128,1536]{1,0:T(8,128)(2,1)}) custom-call(bf16[128,1536]{1,0:T(8,128)(2,1)} %get-tuple-element.16.refs_0_, bf16[128,1536]{1,0:T(8,128)(2,1)} %get-tuple-element.17.refs_1_, bf16[128,1536]{1,0:T(8,128)(2,1)} %get-tuple-element.18.refs_2_, ...), custom_call_target="tpu_custom_call" | custom-call | tf_op jit(solution)/shard_map/pallas_call | solution.py:487
  128.7 0.0 copy-start.1
  128.8 0.6 copy-done.1
  129.3 0.0 copy-start
  129.3 0.5 copy.15
  129.8 0.2 copy-done
  130.0 0.5 copy.16
Async XLA Ops:
  128.7 0.6 copy-start.1
  129.3 0.7 copy-start

commit v3 on v2

--- a/solution.py
+++ b/solution.py
@@ -13,7 +13,8 @@
 CLOSED = -1e30
 MESH = pl.DeviceIdType.MESH
 V, K, D, Q = 0, 1, 2, 3
-UNROLL = 4
+UNROLL = 3
+HALVES = 2
 
 
 def dot_nt(left, right):
@@ -58,10 +59,10 @@
     k_hbm,
     v_hbm,
     d_hbm,
-    out_ref,
-    qg_ref,
-    kg_ref,
-    vg_ref,
+    out_hbm,
+    qg_hbm,
+    kg_hbm,
+    vg_hbm,
     q_part_ref,
     k_part_ref,
     near,
@@ -71,8 +72,13 @@
     gains,
     q_ref,
     k_ref,
+    out_ref,
+    qg_ref,
+    kg_ref,
+    vg_ref,
     sums,
     load_sem,
+    save_sem,
     gain_send,
     gain_recv,
     sum_send,
@@ -84,6 +90,9 @@
 ):
     fsdp, ty, tx, frames, rows, heads, size, slots = dims
     width = heads * size
+    parts = frames * HALVES
+    group = heads // HALVES
+    wide = group * size
     z = lax.axis_index("fsdp")
     t = lax.axis_index("ty")
     x = lax.axis_index("tx")
@@ -103,10 +112,15 @@
     def greet(device):
         pl.semaphore_signal(barrier, inc=1, device_id=device, device_id_type=MESH)
 
-    lines = (("fsdp", z, fsdp), ("tx", x, tx), ("ty", t, ty))
-    for axis, place_in, count in lines:
-        for step in range(1, count):
-            greet({axis: lax.rem(place_in + step, count)})
+    plane = [
+        ({"ty": lax.rem(t + i, ty), "tx": lax.rem(x + j, tx)})
+        for i in range(ty) for j in range(tx) if i or j
+    ]
+    line = [{"fsdp": lax.rem(z + i, fsdp)} for i in range(1, fsdp)]
+    groups = ((plane, t * tx + x), (line, z))
+    for peers, _ in groups:
+        for peer in peers:
+            greet(peer)
 
     loads = [
         pltpu.make_async_copy(source.at[frame * rows:(frame + 1) * rows], target, load_sem.at[i])
@@ -122,13 +136,14 @@
     def block(buffer, chunk, slot):
         if buffer is stat:
             return stat.at[chunk, slot]
-        array, frame = chunk
-        return near.at[array, frame, pl.ds(slot * rows, rows)]
+        array, part = chunk
+        frame, half = divmod(part, HALVES)
+        return near.at[array, frame, pl.ds(slot * rows, rows), pl.ds(half * wide, wide)]
 
     def sem_index(buffer, chunk):
         if buffer is stat:
-            return 4 * frames + chunk
-        return chunk[0] * frames + chunk[1]
+            return 4 * parts + chunk
+        return chunk[0] * parts + chunk[1]
 
     def x_copy(link, buffer, chunk):
         column, peer, _, _ = link
@@ -197,7 +212,7 @@
     def clear(slot):
         near[:, :, slot * rows:(slot + 1) * rows, :] = jnp.zeros(
             (4, frames, rows, width), near.dtype)
-        stat[:, slot] = jnp.zeros((frames,) + stat.shape[2:], stat.dtype)
+        stat[:, slot] = jnp.zeros((parts,) + stat.shape[2:], stat.dtype)
 
     exists = [None] * slots
     for column in range(slots // 3):
@@ -241,7 +256,7 @@
     gains[z, 1:2, 0:share] = k_gain_ref[...]
     gains[z] = pltpu.roll(gains[z], z * share, 1)
 
-    pl.semaphore_wait(barrier, fsdp + tx + ty - 3)
+    pl.semaphore_wait(barrier, len(plane) + len(line))
 
     def gain_copy(step):
         return pltpu.make_async_remote_copy(
@@ -255,10 +270,12 @@
 
     for step in range(1, fsdp):
         gain_copy(step).start()
-    loads[0].wait()
-    start_x(near, (V, 0))
-    start_ty(near, (V, 0))
-    for load in loads[1:]:
+    for frame in range(frames):
+        loads[frame].wait()
+        for half in range(HALVES):
+            start_x(near, (V, frame * HALVES + half))
+            start_ty(near, (V, frame * HALVES + half))
+    for load in loads[frames:]:
         load.wait()
     for step in range(1, fsdp):
         gain_copy(step).wait()
@@ -267,25 +284,32 @@
     k_gain = gain_all[1:2]
 
     def place(source, array, frame, gain):
-        def one(head, carry):
-            cols = pl.ds(pl.multiple_of(head * size, size), size)
+        for head in range(heads):
+            cols = slice(head * size, (head + 1) * size)
             normed, _ = norm_parts(source[frame * rows:(frame + 1) * rows, cols])
             near[array, frame, 0:rows, cols] = (normed * gain).astype(near.dtype)
-            return carry
-
-        lax.fori_loop(0, heads, one, 0)
-
-    place(k_ref, K, 0, k_gain)
-    start_x(near, (K, 0))
-    start_ty(near, (K, 0))
-    for frame in range(1, frames):
-        start_x(near, (V, frame))
+
+    for frame in range(frames):
         place(k_ref, K, frame, k_gain)
-        start_x(near, (K, frame))
+        for half in range(HALVES):
+            start_x(near, (K, frame * HALVES + half))
+            start_ty(near, (K, frame * HALVES + half))
     for frame in range(frames):
-        start_x(near, (D, frame))
         place(q_ref, Q, frame, q_gain)
-        start_x(near, (Q, frame))
+        for half in range(HALVES):
+            start_x(near, (D, frame * HALVES + half))
+            start_x(near, (Q, frame * HALVES + half))
+
+    def saves(pairs, part):
+        frame, half = divmod(part, HALVES)
+        spot = (pl.ds(frame * rows, rows), pl.ds(half * wide, wide))
+        return [
+            pltpu.make_async_copy(source.at[spot], target.at[spot], save_sem.at[i, part])
+            for i, source, target in pairs
+        ]
+
+    query_saves = [(0, out_ref, out_hbm), (1, qg_ref, qg_hbm)]
+    key_saves = [(2, kg_ref, kg_hbm), (3, vg_ref, vg_hbm)]
 
     stat_lane = lax.broadcasted_iota(jnp.int32, (rows, stat.shape[3]), 1)
 
@@ -296,7 +320,7 @@
         mean = jnp.mean(scaled * normed, axis=-1, keepdims=True)
         return inverse * (scaled - normed * mean), part
 
-    def query_head(frame, head, held, part):
+    def query_head(frame, head, mark, held, part):
         cols = pl.ds(pl.multiple_of(head * size, size), size)
         span = slice(frame * rows, (frame + 1) * rows)
         keys = near[K, frame, :, cols]
@@ -315,25 +339,28 @@
         raw_grad, more = backward(
             q_ref[span, cols], dot_nn(score_grad, keys) * scale, q_gain)
         qg_ref[span, cols] = raw_grad.astype(jnp.bfloat16)
-        held = jnp.where(stat_lane == head, inverse, held)
-        held = jnp.where(stat_lane == 16 + head, delta, held)
+        held = jnp.where(stat_lane == mark, inverse, held)
+        held = jnp.where(stat_lane == 8 + mark, delta, held)
         return held, part + more
 
-    def query_side(frame, part):
+    def query_side(chunk, part):
+        frame, half = divmod(chunk, HALVES)
+
         def some(step, carry):
             held, part = carry
             for k in range(UNROLL):
-                held, part = query_head(frame, step * UNROLL + k, held, part)
+                mark = step * UNROLL + k
+                held, part = query_head(frame, half * group + mark, mark, held, part)
             return held, part
 
         held, part = lax.fori_loop(
-            0, heads // UNROLL, some,
+            0, group // UNROLL, some,
             (jnp.zeros((rows, stat.shape[3]), jnp.float32), part))
         turned = jnp.transpose(jnp.concatenate([held, held], axis=0))
-        stat[frame, 0] = turned[0:stat.shape[2]]
+        stat[chunk, 0] = turned[0:stat.shape[2]]
         return part
 
-    def key_head(frame, head, part):
+    def key_head(frame, head, mark, part):
         cols = pl.ds(pl.multiple_of(head * size, size), size)
         span = slice(frame * rows, (frame + 1) * rows)
         keys = near[K, frame, 0:rows, cols]
@@ -341,66 +368,76 @@
         queries = near[Q, frame, :, cols]
         grads = near[D, frame, :, cols]
         weights = jnp.exp2(dot_nt(keys, queries) * exp_scale + bias[pl.ds(head, 1), :])
-        shares = weights * srow[pl.ds(head, 1), :]
+        shares = weights * srow[pl.ds(mark, 1), :]
         vg_ref[span, cols] = dot_nn(shares.astype(jnp.bfloat16), grads).astype(jnp.bfloat16)
         share_grad = dot_nt(vals, grads)
-        score_grad = (shares * (share_grad - srow[pl.ds(16 + head, 1), :])).astype(jnp.bfloat16)
+        score_grad = (shares * (share_grad - srow[pl.ds(8 + mark, 1), :])).astype(jnp.bfloat16)
         raw_grad, more = backward(
             k_ref[span, cols], dot_nn(score_grad, queries) * scale, k_gain)
         kg_ref[span, cols] = raw_grad.astype(jnp.bfloat16)
         return part + more
 
-    def key_side(frame, part):
+    def key_side(chunk, part):
+        frame, half = divmod(chunk, HALVES)
         side = lax.broadcasted_iota(jnp.int32, (stat.shape[2], 2 * rows), 1)
         for pair in range(slots // 2):
             srow[:, pair * 2 * rows:(pair + 1) * 2 * rows] = jnp.where(
-                side < rows, stat[frame, 2 * pair], stat[frame, 2 * pair + 1])
+                side < rows, stat[chunk, 2 * pair], stat[chunk, 2 * pair + 1])
 
         def some(step, part):
             for k in range(UNROLL):
-                part = key_head(frame, step * UNROLL + k, part)
+                mark = step * UNROLL + k
+                part = key_head(frame, half * group + mark, mark, part)
             return part
 
-        return lax.fori_loop(0, heads // UNROLL, some, part)
-
-    pairs = [(V, K, frame) for frame in range(frames)]
-    pairs += [(D, Q, frame) for frame in range(frames)]
+        return lax.fori_loop(0, group // UNROLL, some, part)
+
+    steps = [(V, K, chunk) for chunk in range(parts)]
+    steps += [(D, Q, chunk) for chunk in range(parts)]
+
+    def forward_step(first, second, chunk):
+        forward(near, (first, chunk))
+        forward(near, (second, chunk))
+        if first == V:
+            start_ty(near, (D, chunk))
+            start_ty(near, (Q, chunk))
+        else:
+            forward(stat, chunk)
+
+    q_part = jnp.zeros((1, size), jnp.float32)
     part = jnp.zeros((1, size), jnp.float32)
-    for place_in, (first, second, frame) in enumerate(pairs):
-        forward(near, (first, frame))
-        forward(near, (second, frame))
-        if place_in + 1 < len(pairs):
-            later = pairs[place_in + 1]
-            start_ty(near, (later[0], later[2]))
-            start_ty(near, (later[1], later[2]))
-        if first == D:
-            forward(stat, frame)
-        arrive(near, (first, frame))
-        arrive(near, (second, frame))
+    forward_step(*steps[0])
+    for place_in, (first, second, chunk) in enumerate(steps):
+        if place_in + 1 < len(steps):
+            forward_step(*steps[place_in + 1])
+        arrive(near, (first, chunk))
+        arrive(near, (second, chunk))
         if first == V:
-            part = query_side(frame, part)
-            start_x(stat, frame)
-            start_ty(stat, frame)
-            if frame == frames - 1:
-                q_part = part
-                part = jnp.zeros((1, size), jnp.float32)
+            q_part = query_side(chunk, q_part)
+            start_x(stat, chunk)
+            start_ty(stat, chunk)
+            for save in saves(query_saves, chunk):
+                save.start()
         else:
-            arrive(stat, frame)
-            part = key_side(frame, part)
+            arrive(stat, chunk)
+            part = key_side(chunk, part)
+            for save in saves(key_saves, chunk):
+                save.start()
     side = lax.broadcasted_iota(jnp.int32, (8, size), 0)
     total = jnp.where(side == 0, q_part, jnp.where(side == 1, part, 0.0))
     first = 0
-    for axis, place_in, count in lines:
+    for peers, place_in in groups:
+        count = len(peers) + 1
         if count > 1:
             sums[first + place_in] = total
 
-            def sum_copy(step, axis=axis, place_in=place_in, count=count, first=first):
+            def sum_copy(step, peers=peers, place_in=place_in, first=first):
                 return pltpu.make_async_remote_copy(
                     src_ref=sums.at[first + place_in],
                     dst_ref=sums.at[first + place_in],
                     send_sem=sum_send.at[first + step],
                     recv_sem=sum_recv.at[first + step],
-                    device_id={axis: lax.rem(place_in + step, count)},
+                    device_id=peers[step - 1],
                     device_id_type=MESH,
                 )
 
@@ -414,20 +451,18 @@
     q_part_ref[...] = owned[0:1, 0:share]
     k_part_ref[...] = owned[1:2, 0:share]
 
-    for frame in range(frames):
+    for chunk in range(parts):
         for array in range(4):
-            finish(near, (array, frame))
-        finish(stat, frame)
+            finish(near, (array, chunk))
+        finish(stat, chunk)
+        for save in saves(query_saves + key_saves, chunk):
+            save.wait()
 
 
 def store(*refs):
-    copies = [
-        pltpu.make_async_copy(refs[i], refs[4 + i], refs[8].at[i]) for i in range(4)
-    ]
-    for copy in copies:
-        copy.start()
-    for copy in copies:
-        copy.wait()
+    count = len(refs) // 2
+    for i in range(count):
+        refs[count + i][...] = refs[i][...]
 
 
 def body(axes, q_raw, k_raw, values, d_out, q_gain, k_gain, windows):
@@ -442,28 +477,28 @@
     flat = (frames * rows, width)
     field = jax.ShapeDtypeStruct(flat, jnp.bfloat16)
     vmem = pl.BlockSpec(memory_space=pltpu.VMEM)
-    sems = 5 * frames
+    sems = 5 * frames * HALVES
     dims = (fsdp, ty, tx, frames, rows, heads, size, slots)
     dma = pltpu.SemaphoreType.DMA
     side = max(columns - 1, 1)
     hbm = pl.BlockSpec(memory_space=pltpu.HBM)
     gain_field = jax.ShapeDtypeStruct((1, share), jnp.float32)
-    peers = fsdp + ty + tx
-    *fields, q_part, k_part = pl.pallas_call(
+    peers = fsdp + ty * tx
+    results = pl.pallas_call(
         functools.partial(kernel, dims),
         out_shape=[field] * 4 + [gain_field] * 2,
         in_specs=[pl.BlockSpec(memory_space=pltpu.SMEM)] + [vmem] * 2 + [hbm] * 4,
-        out_specs=[vmem] * 6,
+        out_specs=[hbm] * 4 + [vmem] * 2,
         scratch_shapes=[
             pltpu.VMEM((4, frames, slots * rows, width), jnp.bfloat16),
-            pltpu.VMEM((frames, slots, 32, 2 * rows), jnp.float32),
-            pltpu.VMEM((32, slots * rows), jnp.float32),
+            pltpu.VMEM((frames * HALVES, slots, 16, 2 * rows), jnp.float32),
+            pltpu.VMEM((16, slots * rows), jnp.float32),
             pltpu.VMEM((16, slots * rows), jnp.float32),
             pltpu.VMEM((fsdp, 8, size), jnp.float32),
-            pltpu.VMEM(flat, jnp.bfloat16),
-            pltpu.VMEM(flat, jnp.bfloat16),
+            *[pltpu.VMEM(flat, jnp.bfloat16) for _ in range(6)],
             pltpu.VMEM((peers, 8, size), jnp.float32),
             dma((4 * frames,)),
+            dma((4, frames * HALVES)),
             dma((max(fsdp - 1, 1),)),
             dma((max(fsdp - 1, 1),)),
             dma((peers,)),
@@ -484,13 +519,16 @@
         values.reshape(flat),
         d_out.reshape(flat),
     )
-    fields = pl.pallas_call(
+    tall = frames * rows // 2
+    blocks = [pl.BlockSpec((tall, width), lambda i: (i, 0))] * 4
+    blocks += [pl.BlockSpec((1, share), lambda i: (0, 0))] * 2
+    *fields, q_part, k_part = pl.pallas_call(
         store,
-        out_shape=[field] * 4,
-        in_specs=[pl.BlockSpec(memory_space=pl.ANY)] * 4,
-        out_specs=[hbm] * 4,
-        scratch_shapes=[dma((4,))],
-    )(*fields)
+        out_shape=[field] * 4 + [gain_field] * 2,
+        grid=(2,),
+        in_specs=blocks,
+        out_specs=blocks,
+    )(*results)
     return tuple(one.reshape(q_raw.shape) for one in fields) + (q_part[0], k_part[0])
 
 

time: 131 us -> 71.8 us (0.55)
  Pallas kernels: 128 us -> 71 us
  local copies, waits for them, and re-layouts: 1.76 us -> 0 us
    pallas_call x1, Pallas kernels: 48.8 us -> 2.43 us  [body(): pl.pallas_call(store, out_shape=[field] * 4 + [gain_field] * 2, grid=(2,)...]
    pallas_call x1, Pallas kernels: 79.3 us -> 68.6 us  [body(): pl.pallas_call(functools.partial(kernel, dims), out_shape=[field] * 4 + [...]
    unnamed x6 -> x0, local copies, waits for them, and re-layouts: 1.76 us -> none
where the time goes in v3:
time: 71.8 us; the launch traced here: 71.6 us
  Pallas kernels  71 us (99%)
    pallas_call x1, Pallas kernels, body(): pl.pallas_call(functools.partial(kernel, dims), out_shape=[field] * 4 + [...  68.6 us
    pallas_call x1, Pallas kernels, body(): pl.pallas_call(store, out_shape=[field] * 4 + [gain_field] * 2, grid=(2,)...  2.43 us

profile of v3, /device:TPU:0, one launch (start us, length us, event | category | flops | bytes accessed | tf_op | source)
XLA Modules:
  0.0 71.6 jit_solution(12996615704927329214)
XLA Ops:
  0.6 68.6 %shard_map.118 = (bf16[128,1536]{1,0:T(8,128)(2,1)}, bf16[128,1536]{1,0:T(8,128)(2,1)}, bf16[128,1536]{1,0:T(8,128)(2,1)}, bf16[128,1536]{1,0:T(8,128)(2,1)}, f32[1,32]{1,0:T(1,128)}, /*index=5*/f32[1,32]{1,0:T(1,128)}) custom-call(s32[2,12]{1,0:T(2,128)} %bitcast.17, f32[1,32]{1,0:T(1,128)} %bitcast.18, f32[1,32]{1,0:T(1,128)} %bitcast.19, ...), custom_call_target="tpu_custom_call" | custom-call | tf_op jit(solution)/shard_map/pallas_call | solution.py:487
  69.2 2.4 %shard_map.119 = (bf16[128,1536]{1,0:T(8,128)(2,1)}, bf16[128,1536]{1,0:T(8,128)(2,1)}, bf16[128,1536]{1,0:T(8,128)(2,1)}, bf16[128,1536]{1,0:T(8,128)(2,1)}, f32[1,32]{1,0:T(1,128)}, /*index=5*/f32[1,32]{1,0:T(1,128)}) custom-call(bf16[128,1536]{1,0:T(8,128)(2,1)} %get-tuple-element.18.refs_0_, bf16[128,1536]{1,0:T(8,128)(2,1)} %get-tuple-element.19.refs_1_, ...), custom_call_target="tpu_custom_call" | custom-call | tf_op jit(solution)/shard_map/pallas_call | solution.py:525
